TPU v7x, 32 devices: a whole 2x2x4 slice. The times are simulated.
32 devices in a mesh: row: 2 (over y), vocab: 16 (over z, x, core).
Axes of the slice: x: 2, y: 2, z: 4, core: 2. Of those that a mesh axis runs over, the one named last changes fastest.
Arguments:
- tokens: bfloat16 [320, 7168], P(('row', 'vocab')), may hold values from -60 to 60
- norm_gain: float32 [7168], replicated, may hold values from 0.5 to 1.5
- router: bfloat16 [7168, 16], replicated, may hold values from -0.0625 to 0.0625
- routes: int32 [320, 8], P(('row', 'vocab')), may hold values from 0 to 15, all different within a row; in each aligned block of 10 rows (0 to 9, 10 to 19, ...) at most 5 rows name the same one
- w_gate: bfloat16 [16, 7168, 1024], P('vocab', None, 'row'), may hold values from -0.0625 to 0.0625
- w_up: bfloat16 [16, 7168, 1024], P('vocab', None, 'row'), may hold values from -0.0625 to 0.0625
- w_down: bfloat16 [16, 1024, 7168], P('vocab', 'row'), may hold values from -0.1875 to 0.1875
- head_gain: float32 [7168], replicated, may hold values from 0.5 to 1.5
- head: bfloat16 [65536, 7168], P(('row', 'vocab')), may hold values from -0.18 to 0.18
- draft_logits: bfloat16 [64, 4, 65536], P(None, None, ('row', 'vocab')), may hold values from -18 to 235
- draft_tokens: int32 [64, 4], replicated, may hold values from 0 to 65535
- reject_pos: int32 [64], replicated, may hold values from 0 to 4
Outputs:
- residual: float32 [64, 65536], P(None, ('row', 'vocab'))
- accept: float32 [64, 4], replicated
Inputs may be any that keep to these rules, and one draw needn't show every extreme that they name: `routes`: each row names 8 different experts. Among the rows of one device no expert is named more than 5 times, and some device's rows name some expert exactly 5 times.
All inputs are finite; a program needn't handle non-finite values.
Results may differ from a plain program's by a relative error of at most 0.012.
Values may be sent and summed in bfloat16 or wider, within the bound.
A program may use at most 256 MiB of HBM per device.

v0:
```python
import jax
import jax.numpy as jnp
from jax import lax
from jax.sharding import PartitionSpec as P

V = 65536
DRAFTS = 4


def rms_norm(values, gain):
    return values * lax.rsqrt(jnp.mean(values * values, axis=-1, keepdims=True) + 1e-06) * gain


def body(
    tokens,
    norm_gain,
    router,
    routes,
    w_gate,
    w_up,
    w_down,
    head_gain,
    head,
    draft_logits,
    draft_tokens,
    reject_pos,
):
    vocab_count = lax.axis_size("vocab")
    rows_dev = tokens.shape[0]
    model_width = tokens.shape[1]
    top_k = routes.shape[1]
    experts = w_gate.shape[0] * vocab_count
    capacity = min(rows_dev, (rows_dev * top_k + experts - 1) // experts)
    ff_part = w_gate.shape[2]
    resid_in = tokens.astype(jnp.float32)
    normed = rms_norm(resid_in, norm_gain).astype(jnp.bfloat16)
    scores = jax.nn.sigmoid(jnp.dot(normed, router, preferred_element_type=jnp.float32))
    member = routes[:, :, None] == jnp.arange(experts, dtype=jnp.int32)[None, None, :]
    chosen = jnp.any(member, axis=1)
    chosen_int = chosen.astype(jnp.int32)
    picked = chosen.astype(jnp.float32) * scores
    weights = 2.5 * picked / jnp.sum(picked, axis=1, keepdims=True)
    earlier = jnp.cumsum(chosen_int, axis=0) - chosen_int
    slot_ids = jnp.arange(capacity, dtype=jnp.int32)[None, :, None]
    selector = ((earlier.T[:, None, :] == slot_ids) & chosen.T[:, None, :]).astype(jnp.float32)
    send_buffer = jnp.einsum(
        "esr,rd->esd", selector.astype(jnp.bfloat16), normed, preferred_element_type=jnp.float32
    ).astype(jnp.bfloat16)
    gate_w = w_gate[0]
    up_w = w_up[0]
    down_w = w_down[0]
    received = lax.all_to_all(send_buffer, "vocab", split_axis=0, concat_axis=0, tiled=True)
    slot_count = received.shape[1]
    shard_piece = lax.all_gather(received, "row", axis=0, tiled=True)
    flat_rows = shard_piece.reshape(-1, model_width)
    gate_out = jnp.dot(flat_rows, gate_w, preferred_element_type=jnp.float32)
    up_out = jnp.dot(flat_rows, up_w, preferred_element_type=jnp.float32)
    hidden_hidden = (jax.nn.silu(gate_out) * up_out).astype(jnp.bfloat16)
    hidden = hidden_hidden.reshape(shard_piece.shape[0], shard_piece.shape[1], ff_part)
    down_out = jnp.dot(hidden.reshape(-1, ff_part), down_w, preferred_element_type=jnp.float32)
    down_out = down_out.astype(jnp.bfloat16).astype(jnp.float32)
    summed = lax.psum_scatter(
        down_out.reshape(received.shape[0] * lax.axis_size("row"), slot_count, model_width).astype(
            jnp.bfloat16
        ),
        "row",
        scatter_dimension=0,
        tiled=True,
    )
    returned = lax.all_to_all(summed, "vocab", split_axis=0, concat_axis=0, tiled=True)
    combine = selector * weights.T[:, None, :]
    moe_sum = jnp.einsum(
        "esr,esd->rd", combine, returned.astype(jnp.float32), precision=lax.Precision.HIGHEST
    )
    mixed_rows = resid_in + moe_sum
    final_normed = rms_norm(mixed_rows, head_gain).astype(jnp.bfloat16)
    local_vocab = head.shape[0]
    logits = lax.dot_general(
        lax.all_gather(final_normed, ("row", "vocab"), axis=0, tiled=True),
        head,
        (((1,), (1,)), ((), ())),
        preferred_element_type=jnp.float32,
    )
    requests = draft_tokens.shape[0]
    slot_total = DRAFTS + 1
    target_logits = logits.reshape(requests, slot_total, local_vocab)
    draft_vals = draft_logits.astype(jnp.float32)
    offset = lax.axis_index(("row", "vocab")) * local_vocab
    local_ids = draft_tokens - offset
    id_match = jnp.arange(local_vocab, dtype=jnp.int32)[None, None, :] == local_ids[:, :, None]
    pick_target = jnp.sum(jnp.where(id_match, target_logits[:, :DRAFTS], 0.0), axis=-1)
    pick_draft = jnp.sum(jnp.where(id_match, draft_vals, 0.0), axis=-1)
    local_top_target = jnp.max(target_logits, axis=-1)
    local_top_draft = jnp.max(draft_vals, axis=-1)
    top_target, top_draft = lax.pmax((local_top_target, local_top_draft), ("row", "vocab"))
    local_sum_target = jnp.sum(jnp.exp(target_logits - top_target[:, :, None]), axis=-1)
    local_sum_draft = jnp.sum(jnp.exp(draft_vals - top_draft[:, :, None]), axis=-1)
    sum_target, sum_draft, pick_t, pick_d = lax.psum(
        (local_sum_target, local_sum_draft, pick_target, pick_draft), ("row", "vocab")
    )
    target = jnp.exp(target_logits - top_target[:, :, None]) / sum_target[:, :, None]
    draft_prob = jnp.exp(draft_vals - top_draft[:, :, None]) / sum_draft[:, :, None]
    log_target = pick_t - top_target[:, :DRAFTS] - jnp.log(sum_target[:, :DRAFTS])
    log_draft = pick_d - top_draft - jnp.log(sum_draft)
    accept = jnp.exp(jnp.minimum(log_target - log_draft, 0.0))
    position = (jnp.arange(slot_total, dtype=jnp.int32)[None, :] == reject_pos[:, None]).astype(
        jnp.float32
    )
    target_at = jnp.sum(position[:, :, None] * target, axis=1)
    draft_at = jnp.sum(position[:, :DRAFTS, None] * draft_prob, axis=1)
    gap_rows = jnp.maximum(target_at - draft_at, 0.0)
    gap_total = lax.psum(jnp.sum(gap_rows, axis=-1), ("row", "vocab"))
    residual = jnp.sqrt(V * gap_rows / gap_total[:, None])
    return (residual, accept)


def solution(mesh):
    placed = (
        P(("row", "vocab"), None),
        P(),
        P(),
        P(("row", "vocab"), None),
        P("vocab", None, "row"),
        P("vocab", None, "row"),
        P("vocab", "row", None),
        P(),
        P(("row", "vocab"), None),
        P(None, None, ("row", "vocab")),
        P(),
        P(),
    )
    return jax.shard_map(
        body,
        mesh=mesh,
        in_specs=placed,
        out_specs=(P(None, ("row", "vocab")), P()),
        check_vma=False,
    )
```

profile of v0, /device:TPU:0, one launch (start us, length us, event | category | flops | bytes accessed | tf_op | source)
XLA Modules:
  0.0 468.1 jit_solution(4794459756496341690)
XLA Ops:
  8.2 1.1 fusion.25
  9.3 1.5 convolution_convert_fusion.1
  11.4 49.9 %all_to_all.10 = bf16[16,5,7168]{2,1,0:T(8,128)(2,1)S(1)} all-to-all(bf16[16,5,7168]{2,1,0:T(8,128)(2,1)S(1)} %copy.44), channel_id=1, replica_groups=mesh['row'=2,'vocab'=16] {'vocab'}, dimensions={0} | all-to-all | bytes 2293760 | tf_op jit(solution)/shard_map/all_to_all | solution.py:52
  61.4 1.8 copy.45
  63.2 34.8 %all-gather.4.cloned.1.call-done = bf16[32,5,7168]{2,0,1:T(8,128)(2,1)} async-done(((bf16[16,5,7168]{2,0,1:T(8,128)(2,1)}), bf16[32,5,7168]{2,0,1:T(8,128)(2,1)}) %all-gather.4.cloned.1.call-update) | async-done | bytes 2293776 | tf_op jit(solution)/shard_map/all_gather | solution.py:54
  98.0 4.8 %copy.46 = bf16[32,5,7168]{2,1,0:T(8,128)(2,1)} copy(bf16[32,5,7168]{2,0,1:T(8,128)(2,1)} %all-gather.4.cloned.1.call-done) | data formatting | bytes 4587520 | tf_op jit(solution)/shard_map/all_gather | solution.py:54
  102.7 3.3 reshape.67
  106.0 4.4 fusion.4
  110.4 9.2 %convolution_convert_fusion = bf16[160,7168]{1,0:T(8,128)(2,1)} fusion(bf16[1,512,7168]{2,1,0:T(8,128)(2,1)} %param.18, bf16[160,7168]{1,0:T(8,128)(2,1)S(1)} %reshape.67, bf16[1,7168,512]{2,1,0:T(8,128)(2,1)} %param.17, f32[160,512]{1,0:T(8,128)S(1)} %fusion.4), kind=kOutput, calls=%fused_computation | convolution fusion | flops 2350448640 | bytes 19595264 | tf_op jit(solution)/shard_map/dot_general | solution.py:60
  119.7 4.6 convert_element_type.57
  124.3 49.2 %reduce-scatter.2.cloned.1.call-done = bf16[16,5,7168]{2,1,0:T(8,128)(2,1)} async-done(((bf16[32,5,7168]{2,1,0:T(8,128)(2,1)}), bf16[16,5,7168]{2,1,0:T(8,128)(2,1)}) %reduce-scatter.2.cloned.1.call-update) | async-done | bytes 1146896 | tf_op jit(solution)/shard_map/reduce_scatter | solution.py:62
  173.5 5.6 %all-to-all-start.1 = ((bf16[16,5,7168]{2,1,0:T(8,128)(2,1)}), bf16[16,5,7168]{2,1,0:T(8,128)(2,1)S(1)}, u32[]{:S(2)}, u32[]{:S(2)}) async-start(bf16[16,5,7168]{2,1,0:T(8,128)(2,1)} %reduce-scatter.2.cloned.1.call-done), calls=%async_computation.2 | async-start | bytes 3670016 | tf_op jit(solution)/shard_map/all_to_all | solution.py:70
  179.9 35.8 %all-to-all-done.1 = bf16[16,5,7168]{2,1,0:T(8,128)(2,1)S(1)} async-done(((bf16[16,5,7168]{2,1,0:T(8,128)(2,1)}), bf16[16,5,7168]{2,1,0:T(8,128)(2,1)S(1)}, u32[]{:S(2)}, u32[]{:S(2)}) %all-to-all-start.1) | async-done | bytes 1146912 | tf_op jit(solution)/shard_map/all_to_all | solution.py:70
  215.7 2.0 multiply_reduce_fusion.1
  219.2 77.5 %all-gather.6.cloned.1.call-done = bf16[32,10,7168]{2,1,0:T(8,128)(2,1)} async-done(((bf16[1,10,7168]{2,1,0:T(8,128)(2,1)}), bf16[32,10,7168]{2,1,0:T(8,128)(2,1)}) %all-gather.6.cloned.1.call-update) | async-done | bytes 4587536 | tf_op jit(solution)/shard_map/all_gather | solution.py:79
  296.7 8.1 %reshape.70 = bf16[320,7168]{1,0:T(8,128)(2,1)} reshape(bf16[32,10,7168]{2,1,0:T(8,128)(2,1)} %all-gather.6.cloned.1.call-done) | data formatting | bytes 9175040
  304.8 15.6 %fusion.58 = (f32[320]{0:T(512)S(1)}, f32[320,2048]{1,0:T(8,128)S(1)}) fusion(bf16[320,7168]{1,0:T(8,128)(2,1)} %reshape.70, bf16[2048,7168]{1,0:T(8,128)(2,1)} %param.20), kind=kOutput, calls=%fused_computation.77 | convolution fusion | flops 9395896320 | bytes 36570368 | tf_op jit(solution)/shard_map/dot_general | solution.py:78
  320.5 39.7 %all-reduce.2 = (f32[64,5]{1,0:T(8,128)S(1)}, f32[64,4]{1,0:T(8,128)S(1)}) all-reduce(f32[64,5]{1,0:T(8,128)S(1)} %reduce_max.26, bf16[64,4]{1,0:T(8,128)(2,1)S(1)} %reduce_max.27), channel_id=1, replica_groups=mesh['row'=2,'vocab'=16] {'row','vocab'}, use_global_device_ids=true, to_apply=%region_7.8 | all-reduce | flops 576 | bytes 4096 | tf_op jit(solution)/shard_map/pmax | solution.py:95
  360.3 2.1 reshape.68
  363.1 2.3 fusion.8
  365.4 40.6 %all-reduce.1 = (f32[64,5]{1,0:T(8,128)S(1)}, f32[64,4]{1,0:T(8,128)S(1)}) all-reduce(f32[64,5]{1,0:T(8,128)S(1)} %reduce_sum.96, f32[64,4]{1,0:T(8,128)S(1)} %fusion.8), channel_id=1, replica_groups=mesh['row'=2,'vocab'=16] {'row','vocab'}, use_global_device_ids=true, to_apply=%region_9.10 | all-reduce | flops 576 | bytes 4608 | tf_op jit(solution)/shard_map/psum | solution.py:98
  406.1 8.9 %multiply_reduce_fusion = f32[64,2048]{1,0:T(8,128)S(1)} fusion(f32[64,5,2048]{2,1,0:T(8,128)} %reshape.68, f32[64,5]{1,0:T(8,128)S(1)} %get-tuple-element.16, f32[64,5]{1,0:T(8,128)S(1)} %get-tuple-element.18, f32[64,5]{1,0:T(8,128)S(1)} %fusion.47), kind=kLoop, calls=%fused_computation.9 | loop fusion | flops 2490368 | bytes 3149568 | tf_op jit(solution)/shard_map/reduce_sum | solution.py:109
  415.0 3.7 fusion.10
  418.9 41.0 %all-reduce = (f32[64]{0:T(128)S(1)}, f32[64,4]{1,0:T(8,128)S(1)}, f32[64,4]{1,0:T(8,128)S(1)}) all-reduce(f32[64]{0:T(128)S(1)} %fusion.35, f32[64,4]{1,0:T(8,128)S(1)} %get-tuple-element.12, f32[64,4]{1,0:T(8,128)S(1)} %get-tuple-element.10), channel_id=1, replica_groups=mesh['row'=2,'vocab'=16] {'row','vocab'}, use_global_device_ids=true, to_apply=%region_17.18 | all-reduce | flops 576 | bytes 4608 | tf_op jit(solution)/shard_map/psum | solution.py:112
  (49 shorter events, 6.8 us)
Async XLA Ops:
  7.2 172.2 %copy-start = (bf16[7168,16]{0,1:T(8,128)(2,1)S(1)}, bf16[7168,16]{0,1:T(8,128)(2,1)}, u32[]{:S(2)}) copy-start(bf16[7168,16]{0,1:T(8,128)(2,1)} %param.14) | copy-start | bytes 688132
  7.2 90.8 %all-gather.4.cloned.1.call-start = ((), (), s32[]{:S(2)}) async-start(), calls=%async_computation.3 | async-start | bytes 3440640 | tf_op jit(solution)/shard_map/all_gather | solution.py:54
  63.1 110.4 %reduce-scatter.2.cloned.1.call-start = ((), (), s32[]{:S(2)}) async-start(), calls=%async_computation.4 | async-start | bytes 5505024 | tf_op jit(solution)/shard_map/reduce_scatter | solution.py:62
  124.3 55.2 %copy-start.5 = (bf16[10,7168]{1,0:T(8,128)(2,1)S(1)}, bf16[10,7168]{1,0:T(8,128)(2,1)}, u32[]{:S(2)}) copy-start(bf16[10,7168]{1,0:T(8,128)(2,1)} %param.12) | copy-start | bytes 430084
  124.3 55.2 %copy-start.6 = (f32[7168]{0:T(1024)S(1)}, f32[7168]{0:T(1024)}, u32[]{:S(2)}) copy-start(f32[7168]{0:T(1024)} %param.13) | copy-start | bytes 86020
  124.3 93.4 %copy-start.7 = (f32[7168]{0:T(1024)S(1)}, f32[7168]{0:T(1024)}, u32[]{:S(2)}) copy-start(f32[7168]{0:T(1024)} %param.19) | copy-start | bytes 86020
  173.5 42.2 %all-to-all-start.1 = ((bf16[16,5,7168]{2,1,0:T(8,128)(2,1)}), bf16[16,5,7168]{2,1,0:T(8,128)(2,1)S(1)}, u32[]{:S(2)}, u32[]{:S(2)}) async-start(bf16[16,5,7168]{2,1,0:T(8,128)(2,1)} %reduce-scatter.2.cloned.1.call-done), calls=%async_computation.2 | async-start | bytes 3670016 | tf_op jit(solution)/shard_map/all_to_all | solution.py:70
  179.1 39.4 %copy-start.8 = (s32[64,4]{0,1:T(4,128)S(1)}, s32[64,4]{0,1:T(4,128)}, u32[]{:S(2)}) copy-start(s32[64,4]{0,1:T(4,128)} %param.22) | copy-start | bytes 3076
  179.2 39.5 %copy-start.3 = (bf16[64,4,2048]{2,1,0:T(4,128)(2,1)S(1)}, bf16[64,4,2048]{2,1,0:T(4,128)(2,1)}, u32[]{:S(2)}) copy-start(bf16[64,4,2048]{2,1,0:T(4,128)(2,1)} %param.21) | copy-start | bytes 3145732
  179.2 40.0 %copy-start.9 = (s32[64]{0:T(128)S(1)}, s32[64]{0:T(128)}, u32[]{:S(2)}) copy-start(s32[64]{0:T(128)} %param.23) | copy-start | bytes 772
  179.2 117.5 %all-gather.6.cloned.1.call-start = ((), (), s32[]{:S(2)}) async-start(), calls=%async_computation.5 | async-start | bytes 7569408 | tf_op jit(solution)/shard_map/all_gather | solution.py:79
  363.1 51.9 %copy-start.4 = (bf16[64,4,2048]{2,1,0:T(4,128)(2,1)S(1)}, bf16[64,4,2048]{2,1,0:T(4,128)(2,1)}, u32[]{:S(2)}) copy-start(bf16[64,4,2048]{2,1,0:T(4,128)(2,1)} %param.21) | copy-start | bytes 3145732
  406.1 9.0 %copy-start.2 = (f32[64,5,2048]{2,1,0:T(8,128)S(1)}, f32[64,5,2048]{2,1,0:T(8,128)}, u32[]{:S(2)}) copy-start(f32[64,5,2048]{2,1,0:T(8,128)} %reshape.68) | copy-start | bytes 7864324
  415.0 46.5 %copy-start.1 = (bf16[7168,16]{0,1:T(8,128)(2,1)S(1)}, bf16[7168,16]{0,1:T(8,128)(2,1)}, u32[]{:S(2)}) copy-start(bf16[7168,16]{0,1:T(8,128)(2,1)} %param.14) | copy-start | bytes 688132
Sparse Core Ops, SparseCore 0:
  63.3 34.6 all-gather.3
  124.4 49.0 reduce-scatter.1
  218.6 78.0 all-gather.5
where the time goes:
time: 469 us; the launch traced here: 468 us
  waiting for transfers between devices  197 us (42%)
  blocking collectives  171 us (36%)
  matrix products  33 us (7%)
  local copies, waits for them, and re-layouts  27.3 us (6%)
  other arithmetic  19.3 us (4%)
  between operations  14 us (3%)
  starting transfers between devices  5.92 us (1%)
    all_gather x1, waiting for transfers between devices, body(): lax.all_gather(final_normed, ('row', 'vocab'), axis=0, tiled=True)  77.5 us
    all_to_all x1, blocking collectives, body(): lax.all_to_all(send_buffer, 'vocab', split_axis=0, concat_axis=0, tiled=T...  49.9 us
    reduce_scatter x1, waiting for transfers between devices, body(): lax.psum_scatter(down_out.reshape(received.shape[0] * lax.axis_size('row'...  49.2 us
    psum x1, blocking collectives, body(): gap_total = lax.psum(jnp.sum(gap_rows, axis=-1), ('row', 'vocab'))  41 us
    psum x1, blocking collectives, body(): lax.psum((local_sum_target, local_sum_draft, pick_target, pick_draft), ('...  40.6 us
    pmax x1, blocking collectives, body(): lax.pmax((local_top_target, local_top_draft), ('row', 'vocab'))  39.7 us
    all_to_all x1, waiting for transfers between devices, body(): lax.all_to_all(summed, 'vocab', split_axis=0, concat_axis=0, tiled=True)  35.8 us
    all_gather x1, waiting for transfers between devices, body(): shard_piece = lax.all_gather(received, 'row', axis=0, tiled=True)  34.8 us
  transfers between devices with their start and end apart: 4, of which 4 were waited for; matrix products, arithmetic and copies ran while one was open for 0% of the time, Pallas kernels for 0%

commit v1 on v0

v1 whole, which is shorter than its diff:
```python
import functools

import jax
import jax.numpy as jnp
from jax import lax
from jax.experimental import pallas as pl
from jax.experimental.pallas import tpu as pltpu
from jax.sharding import PartitionSpec as P

V = 65536
DRAFTS = 4
MESH = pl.DeviceIdType.MESH
VMEM = pltpu.VMEM
Z = 4
CHIPS = 16
CUT = 2304


def rms_norm(values, gain):
    return values * lax.rsqrt(jnp.mean(values * values, axis=-1, keepdims=True) + 1e-06) * gain


def place():
    y = lax.axis_index("row")
    v = lax.axis_index("vocab")
    return y, v // 4, (v // 2) % 2, v % 2


def device(y, z, x, c):
    return (y, (z * 2 + x) * 2 + c)


def offset_of(k):
    return ((k + 1) // 2) * (1 - 2 * ((k + 1) % 2))


def greet():
    y, z, x, c = place()
    barrier = pltpu.get_barrier_semaphore()

    def signal(target):
        pl.semaphore_signal(barrier, inc=1, device_id=target, device_id_type=MESH)

    signal(device(y, z, x, 1 - c))
    signal(device(1 - y, z, x, c))
    signal(device(y, z, 1 - x, c))
    pl.when(z + 1 < Z)(lambda: signal(device(y, z + 1, x, c)))
    pl.when(z >= 1)(lambda: signal(device(y, z - 1, x, c)))
    pl.semaphore_wait(barrier, 3 + (z + Z - 1) // Z + (2 * Z - 2 - z) // Z)


def gather_kernel(width, x_ref, o_ref, send_sem, recv_sem):
    y, z, x, c = place()
    halves = (pl.ds(0, CUT), pl.ds(CUT, width - CUT))
    o_ref[y * 8 + z * 2 + x, c] = x_ref[...]
    greet()

    def copy(q, core, h, way, target, stream):
        tile = o_ref.at[q, core, :, halves[h]]
        return pltpu.make_async_remote_copy(
            src_ref=tile,
            dst_ref=tile,
            send_sem=send_sem.at[q, h, way],
            recv_sem=recv_sem.at[q, h, stream],
            device_id=target,
            device_id_type=MESH,
        )

    other = device(y, z, x, 1 - c)

    def visit(k, drain):
        dz = offset_of(k)
        zs = z + dz

        def run(q, h, way, target):
            made = copy(q, c, h, way, target, 1 if way == 0 else 0)
            if drain:
                made.wait_send()
            else:
                made.start()

        @pl.when((zs >= 0) & (zs < Z))
        def _():
            for fx, fy in ((0, 0), (0, 1), (1, 0), (1, 1)):
                q = (1 - y if fy else y) * 8 + zs * 2 + (1 - x if fx else x)
                for h in (0, 1):
                    if not drain:
                        landed = copy(q, c, h, 0, other, 0)
                        if fx or fy:
                            landed.wait_recv()
                        else:
                            pl.when(dz != 0)(landed.wait_recv)
                    if not fx and not fy:
                        pl.when((dz >= 0) & (z >= 1))(lambda: run(q, h, 4, device(y, z - 1, x, c)))
                        pl.when((dz <= 0) & (z + 1 < Z))(lambda: run(q, h, 3, device(y, z + 1, x, c)))
                    if not fy and (h == 0 or not fx):
                        run(q, h, 1, device(1 - y, z, x, c))
                    if not fx and (h == 1 or not fy):
                        run(q, h, 2, device(y, z, 1 - x, c))
                    run(q, h, 0, other)
                    if drain:
                        copy(q, 1 - c, h, 0, other, 1).wait_recv()

    @pl.loop(0, 2 * Z - 1)
    def _(k):
        visit(k, False)

    @pl.loop(0, 2 * Z - 1)
    def _(k):
        visit(k, True)


def gather(block, cid):
    count = lax.axis_size("row") * lax.axis_size("vocab")
    if (lax.axis_size("row"), lax.axis_size("vocab")) != (2, 16):
        return lax.all_gather(block, ("row", "vocab"), axis=0, tiled=False)
    width = block.shape[1]
    out = pl.pallas_call(
        functools.partial(gather_kernel, width),
        out_shape=jax.ShapeDtypeStruct((CHIPS, 2, 16, width), block.dtype),
        in_specs=[pl.BlockSpec(memory_space=VMEM)],
        out_specs=pl.BlockSpec(memory_space=VMEM),
        scratch_shapes=[
            pltpu.SemaphoreType.DMA((CHIPS, 2, 5)),
            pltpu.SemaphoreType.DMA((CHIPS, 2, 2)),
        ],
        compiler_params=pltpu.CompilerParams(
            collective_id=cid, has_side_effects=True, vmem_limit_bytes=40 * 2**20
        ),
    )(block)
    return out.reshape(count, 16, width)


def scatter_kernel(width, p_ref, o_ref, buf, stage, acc, send_sem, recv_sem):
    y, z, x, c = place()
    halves = (pl.ds(0, CUT), pl.ds(CUT, width - CUT))
    sizes = (CUT, width - CUT)
    other = device(y, z, x, 1 - c)
    greet()

    def chip(zs, fx, fy):
        return (1 - y if fy else y) * 8 + zs * 2 + (1 - x if fx else x)

    def to_core(q, h):
        return pltpu.make_async_remote_copy(
            src_ref=p_ref.at[q, 1 - c, :, halves[h]],
            dst_ref=buf.at[0, q, :, halves[h]],
            send_sem=send_sem.at[q, h, 0],
            recv_sem=recv_sem.at[q, h, 0],
            device_id=other,
            device_id_type=MESH,
        )

    def to_parent(q, h, way, target):
        return pltpu.make_async_remote_copy(
            src_ref=stage.at[q, :, halves[h]],
            dst_ref=buf.at[way, q, :, halves[h]],
            send_sem=send_sem.at[q, h, 1],
            recv_sem=recv_sem.at[q, h, way],
            device_id=target,
            device_id_type=MESH,
        )

    flips = ((1, 1), (1, 0), (0, 1), (0, 0))

    def visit(i, phase):
        dz = offset_of(2 * Z - 2 - i)
        zs = z + dz

        @pl.when((zs >= 0) & (zs < Z))
        def _():
            for fx, fy in flips:
                q = chip(zs, fx, fy)
                for h in (0, 1):
                    if phase == 0:
                        to_core(q, h).start()
                        continue
                    if phase == 1:
                        cols = pl.ds(0, sizes[h])

                        def add(way):
                            to_parent(q, h, way, other).wait_recv()
                            acc[:, cols] += buf[way, q, :, halves[h]].astype(jnp.float32)

                        to_core(q, h).wait_recv()
                        acc[:, cols] = p_ref[q, c, :, halves[h]].astype(jnp.float32) + buf[
                            0, q, :, halves[h]
                        ].astype(jnp.float32)
                        if not fy and (h == 0 or not fx):
                            add(1)
                        if not fx and (h == 1 or not fy):
                            add(2)
                        if not fx and not fy:
                            pl.when((dz >= 0) & (z >= 1))(lambda: add(4))
                            pl.when((dz <= 0) & (z + 1 < Z))(lambda: add(3))

                            @pl.when(dz == 0)
                            def _():
                                o_ref[:, halves[h]] = acc[:, cols]

                        stage[q, :, halves[h]] = acc[:, cols].astype(jnp.bfloat16)
                    else:
                        to_core(q, h).wait_send()

                    def run(way, target):
                        made = to_parent(q, h, way, target)
                        if phase == 1:
                            made.start()
                        else:
                            made.wait_send()

                    if fy and (h == 0 or not fx):
                        run(1, device(1 - y, z, x, c))
                    elif fx:
                        run(2, device(y, z, 1 - x, c))
                    else:
                        pl.when(dz > 0)(lambda: run(4, device(y, z + 1, x, c)))
                        pl.when(dz < 0)(lambda: run(3, device(y, z - 1, x, c)))

    for phase in (0, 1, 2):
        pl.loop(0, 2 * Z - 1)(functools.partial(lambda p, i: visit(i, p), phase))


def scatter(parts, cid):
    if (lax.axis_size("row"), lax.axis_size("vocab")) != (2, 16):
        return lax.psum_scatter(
            parts.astype(jnp.float32), ("row", "vocab"), scatter_dimension=0, tiled=False
        )
    width = parts.shape[2]
    return pl.pallas_call(
        functools.partial(scatter_kernel, width),
        out_shape=jax.ShapeDtypeStruct((16, width), jnp.float32),
        in_specs=[pl.BlockSpec(memory_space=VMEM)],
        out_specs=pl.BlockSpec(memory_space=VMEM),
        scratch_shapes=[
            VMEM((5, CHIPS, 16, width), jnp.bfloat16),
            VMEM((CHIPS, 16, width), jnp.bfloat16),
            VMEM((16, CUT), jnp.float32),
            pltpu.SemaphoreType.DMA((CHIPS, 2, 2)),
            pltpu.SemaphoreType.DMA((CHIPS, 2, 5)),
        ],
        compiler_params=pltpu.CompilerParams(
            collective_id=cid, has_side_effects=True, vmem_limit_bytes=40 * 2**20
        ),
    )(parts.reshape(CHIPS, 2, 16, width))


def exchange_kernel(n_vocab, count, x_ref, o_ref, send_sem, recv_sem):
    me = lax.axis_index("row") * n_vocab + lax.axis_index("vocab")
    barrier = pltpu.get_barrier_semaphore()

    @pl.loop(1, count)
    def _(k):
        peer = (me + k) % count
        pl.semaphore_signal(
            barrier, inc=1, device_id=(peer // n_vocab, peer % n_vocab), device_id_type=MESH
        )

    o_ref[me] = x_ref[...]
    pl.semaphore_wait(barrier, count - 1)

    def copy(k, slot):
        peer = (me + k) % count
        return pltpu.make_async_remote_copy(
            src_ref=x_ref,
            dst_ref=o_ref.at[slot],
            send_sem=send_sem.at[k],
            recv_sem=recv_sem.at[k],
            device_id=(peer // n_vocab, peer % n_vocab),
            device_id_type=MESH,
        )

    @pl.loop(1, count)
    def _(k):
        copy(k, me).start()

    @pl.loop(1, count)
    def _(k):
        copy(k, (me + count - k) % count).wait_recv()
        copy(k, me).wait_send()


def exchange(values, cid):
    size = values.shape[0]
    if (lax.axis_size("row"), lax.axis_size("vocab")) != (2, 16):
        return lax.all_gather(values, ("row", "vocab"), axis=0, tiled=False)
    n_vocab = lax.axis_size("vocab")
    count = lax.axis_size("row") * n_vocab
    rows = -(-size // 1024) * 8
    block = jnp.pad(values, (0, rows * 128 - size)).reshape(rows, 128)
    out = pl.pallas_call(
        functools.partial(exchange_kernel, n_vocab, count),
        out_shape=jax.ShapeDtypeStruct((count, rows, 128), jnp.float32),
        in_specs=[pl.BlockSpec(memory_space=VMEM)],
        out_specs=pl.BlockSpec(memory_space=VMEM),
        scratch_shapes=[
            pltpu.SemaphoreType.DMA((count,)),
            pltpu.SemaphoreType.DMA((count,)),
        ],
        compiler_params=pltpu.CompilerParams(collective_id=cid, has_side_effects=True),
    )(block)
    return out.reshape(count, rows * 128)[:, :size]


def pack(rows):
    lead, width = rows.shape[:-2], rows.shape[-1]
    first = rows[..., :8, :]
    main = jnp.concatenate([first[..., : width // 2], first[..., width // 2 :]], axis=-2)
    rest = rows[..., 8:, :].reshape(lead + (16, width // 8))
    return jnp.concatenate([main, rest], axis=-1)


def spread(blocks, width):
    count = blocks.shape[0]
    half = width // 2
    main = jnp.concatenate(
        [blocks[:, :8, :half].reshape(-1, half), blocks[:, 8:, :half].reshape(-1, half)], axis=1
    )
    rest = blocks[:, :, half : half + width // 8].reshape(count * 2, width)
    return jnp.concatenate([main, rest], axis=0)


def unspread(rows, count):
    width = rows.shape[1]
    half = width // 2
    first = rows[: count * 8].reshape(count, 8, width)
    main = jnp.concatenate([first[:, :, :half], first[:, :, half:]], axis=1)
    rest = rows[count * 8 :].reshape(count, 16, width // 8)
    return jnp.concatenate([main, rest], axis=2)


def in_order(per_row, count):
    table = per_row.reshape(count, 10)
    return jnp.concatenate([table[:, :8].reshape(-1), table[:, 8:].reshape(-1)])


def body(
    tokens,
    norm_gain,
    router,
    routes,
    w_gate,
    w_up,
    w_down,
    head_gain,
    head,
    draft_logits,
    draft_tokens,
    reject_pos,
):
    n_vocab = lax.axis_size("vocab")
    count = lax.axis_size("row") * n_vocab
    width = tokens.shape[1]
    packed = width * 5 // 8
    experts = n_vocab
    resid_in = tokens.astype(jnp.float32)
    normed = rms_norm(resid_in, norm_gain).astype(jnp.bfloat16)
    scores = jax.nn.sigmoid(jnp.dot(normed, router, preferred_element_type=jnp.float32))
    member = routes[:, :, None] == jnp.arange(experts, dtype=jnp.int32)[None, None, :]
    picked = jnp.any(member, axis=1).astype(jnp.float32) * scores
    weights = 2.5 * picked / jnp.sum(picked, axis=1, keepdims=True)
    high = lax.reduce_precision(weights, 8, 7)
    low = weights - high
    both = jnp.concatenate([high, low], axis=1).astype(jnp.bfloat16)
    both = jnp.pad(both, ((0, 6), (0, 128 - 2 * experts)))
    gathered = gather(jnp.concatenate([pack(normed), both], axis=1), 0)

    x = spread(gathered, width)
    table = gathered[:, :10, packed : packed + 2 * experts].astype(jnp.float32)
    table = table[:, :, :experts] + table[:, :, experts:]
    mine = jnp.arange(experts, dtype=jnp.int32) == lax.axis_index("vocab")
    row_weight = jnp.sum(jnp.where(mine[None, None, :], table, 0.0), axis=-1)
    row_weight = in_order(row_weight.reshape(-1), count)

    gate_out = jnp.dot(x, w_gate[0], preferred_element_type=jnp.float32)
    up_out = jnp.dot(x, w_up[0], preferred_element_type=jnp.float32)
    hidden = (jax.nn.silu(gate_out) * up_out).astype(jnp.bfloat16)
    down_out = jnp.dot(hidden, w_down[0], preferred_element_type=jnp.float32)
    parts = (down_out * row_weight[:, None]).astype(jnp.bfloat16)
    summed = scatter(unspread(parts, count), 1)

    half = width // 2
    moe_sum = jnp.concatenate(
        [
            jnp.concatenate([summed[:8, :half], summed[8:, :half]], axis=1),
            summed[:, half:].reshape(2, width),
        ],
        axis=0,
    )
    mixed_rows = resid_in + moe_sum
    final_normed = rms_norm(mixed_rows, head_gain).astype(jnp.bfloat16)
    hn = spread(gather(pack(final_normed), 2), width)
    logits = lax.dot_general(
        hn, head, (((1,), (1,)), ((), ())), preferred_element_type=jnp.float32
    )

    local_vocab = head.shape[0]
    requests = draft_tokens.shape[0]
    slots = DRAFTS + 1
    rows = requests * slots
    drafts = requests * DRAFTS
    draft_vals = draft_logits.astype(jnp.float32)
    offset = lax.axis_index(("row", "vocab")) * local_vocab
    lanes = jnp.arange(local_vocab, dtype=jnp.int32)
    local_ids = draft_tokens - offset
    row_ids = in_order(jnp.pad(local_ids, ((0, 0), (0, 1)), constant_values=-1).reshape(-1), count)
    pick_t = jnp.sum(jnp.where(lanes[None, :] == row_ids[:, None], logits, 0.0), axis=-1)
    pick_d = jnp.sum(
        jnp.where(lanes[None, None, :] == local_ids[:, :, None], draft_vals, 0.0), axis=-1
    )
    top_t = jnp.max(logits, axis=-1)
    top_d = jnp.max(draft_vals, axis=-1)
    sum_t = jnp.sum(jnp.exp(logits - top_t[:, None]), axis=-1)
    sum_d = jnp.sum(jnp.exp(draft_vals - top_d[:, :, None]), axis=-1)
    own = [top_t, sum_t, pick_t, top_d.reshape(-1), sum_d.reshape(-1), pick_d.reshape(-1)]
    every = exchange(jnp.concatenate(own), 3)

    def merge(start, size):
        tops = every[:, start : start + size]
        sums = every[:, start + size : start + 2 * size]
        picks = every[:, start + 2 * size : start + 3 * size]
        top = jnp.max(tops, axis=0)
        return top, jnp.sum(sums * jnp.exp(tops - top[None, :]), axis=0), jnp.sum(picks, axis=0)

    top_target, sum_target, pick_target = merge(0, rows)
    top_draft, sum_draft, pick_draft = [
        part.reshape(requests, DRAFTS) for part in merge(3 * rows, drafts)
    ]
    log_draft = pick_draft - top_draft - jnp.log(sum_draft)

    row_at = jnp.arange(requests, dtype=jnp.int32) * slots + reject_pos
    natural = jnp.arange(rows, dtype=jnp.int32)
    order = in_order(natural, count)
    chosen = (row_at[:, None] == order[None, :]).astype(jnp.float32)
    logits_at = jnp.dot(chosen, logits, precision=lax.Precision.HIGHEST)
    top_at = jnp.sum(chosen * top_target[None, :], axis=1)
    sum_at = jnp.sum(chosen * sum_target[None, :], axis=1)
    log_rows = pick_target - top_target - jnp.log(sum_target)
    log_rows = jnp.concatenate(
        [log_rows[: count * 8].reshape(count, 8), log_rows[count * 8 :].reshape(count, 2)], axis=1
    ).reshape(requests, slots)
    accept = jnp.exp(jnp.minimum(log_rows[:, :DRAFTS] - log_draft, 0.0))

    position = jnp.arange(DRAFTS, dtype=jnp.int32)[None, :] == reject_pos[:, None]
    draft_raw = jnp.sum(jnp.where(position[:, :, None], draft_vals, 0.0), axis=1)
    top_d_at = jnp.sum(jnp.where(position, top_draft, 0.0), axis=1)
    sum_d_at = jnp.sum(jnp.where(position, sum_draft, 0.0), axis=1)
    drafted = (reject_pos < DRAFTS)[:, None]
    draft_at = jnp.where(
        drafted, jnp.exp(draft_raw - top_d_at[:, None]) / jnp.where(drafted, sum_d_at[:, None], 1.0), 0.0
    )
    target_at = jnp.exp(logits_at - top_at[:, None]) / sum_at[:, None]
    gap_rows = jnp.maximum(target_at - draft_at, 0.0)
    gap_total = jnp.sum(exchange(jnp.sum(gap_rows, axis=-1), 4), axis=0)
    residual = jnp.sqrt(V * gap_rows / gap_total[:, None])
    return (residual, accept)


def solution(mesh):
    placed = (
        P(("row", "vocab"), None),
        P(),
        P(),
        P(("row", "vocab"), None),
        P("vocab", None, "row"),
        P("vocab", None, "row"),
        P("vocab", "row", None),
        P(),
        P(("row", "vocab"), None),
        P(None, None, ("row", "vocab")),
        P(),
        P(),
    )
    return jax.shard_map(
        body,
        mesh=mesh,
        in_specs=placed,
        out_specs=(P(None, ("row", "vocab")), P()),
        check_vma=False,
    )
```

time: 469 us -> 227 us (0.48)
  waiting for transfers between devices: 197 us -> 0 us
  blocking collectives: 171 us -> 0 us
  Pallas kernels: 0 us -> 148 us
  between operations: 14 us -> 1.11 us
  starting transfers between devices: 5.92 us -> 0 us
    pallas_call x0 -> x5, Pallas kernels: none -> 148 us  [the longest x2 88.4 us: gather(): pl.pallas_call(functools.partial(gather_kernel, width), out_shape=jax.Sha...]
    all_gather x2 -> x0, waiting for transfers between devices: 112 us -> none  [the longest x1 77.5 us: body(): lax.all_gather(final_normed, ('row', 'vocab'), axis=0, tiled=True)]
    psum x2 -> x0, blocking collectives: 81.6 us -> none  [the longest x1 41 us: body(): gap_total = lax.psum(jnp.sum(gap_rows, axis=-1), ('row', 'vocab'))]
    all_to_all x1 -> x0, blocking collectives: 49.9 us -> none  [body(): lax.all_to_all(send_buffer, 'vocab', split_axis=0, concat_axis=0, tiled=T...]
    reduce_scatter x1 -> x0, waiting for transfers between devices: 49.2 us -> none  [body(): lax.psum_scatter(down_out.reshape(received.shape[0] * lax.axis_size('row'...]
    pmax x1 -> x0, blocking collectives: 39.7 us -> none  [body(): lax.pmax((local_top_target, local_top_draft), ('row', 'vocab'))]
    all_to_all x1 -> x0, waiting for transfers between devices: 35.8 us -> none  [body(): lax.all_to_all(summed, 'vocab', split_axis=0, concat_axis=0, tiled=True)]
    reduce_sum x5 -> x8, other arithmetic: 15.5 us -> 6.45 us  [the longest x1 4.07 us: body(): jnp.sum(jnp.where(lanes[None, None, :] == local_ids[:, :, None], draft_va...]
  transfers between devices with their start and end apart: 4 -> 0, of which waited for: 4 -> 0; matrix products, arithmetic and copies ran while one was open for 0% -> 0% of each run, Pallas kernels for 0% -> 0%
where the time goes in v1:
time: 227 us; the launch traced here: 226 us
  Pallas kernels  148 us (65%)
  matrix products  36.9 us (16%)
  local copies, waits for them, and re-layouts  23.3 us (10%)
  other arithmetic  17.4 us (8%)
    pallas_call x2, Pallas kernels, gather(): pl.pallas_call(functools.partial(gather_kernel, width), out_shape=jax.Sha...  88.4 us
    pallas_call x1, Pallas kernels, scatter(): pl.pallas_call(functools.partial(scatter_kernel, width), out_shape=jax.Sh...  36.9 us
    pallas_call x2, Pallas kernels, exchange(): pl.pallas_call(functools.partial(exchange_kernel, n_vocab, count), out_sh...  22.4 us
    dot_general x1, matrix products, body(): lax.dot_general(hn, head, (((1,), (1,)), ((), ())), preferred_element_typ...  18.7 us
    dot_general x1, matrix products, body(): gate_out = jnp.dot(x, w_gate[0], preferred_element_type=jnp.float32)  6.58 us
    dot_general x1, matrix products, body(): up_out = jnp.dot(x, w_up[0], preferred_element_type=jnp.float32)  5.83 us
    unnamed x25, local copies, waits for them, and re-layouts  5.66 us
    reshape x2, local copies, waits for them, and re-layouts, spread(): blocks[:, :8, :half].reshape(-1, half)  5.62 us

profile of v1, /device:TPU:0, one launch (start us, length us, event | category | flops | bytes accessed | tf_op | source)
XLA Modules:
  0.0 226.4 jit_solution(2889772793582594767)
XLA Ops:
  1.4 1.1 fusion.30
  2.5 1.2 broadcast_compare_fusion
  6.0 1.7 reduce_max.46
  8.6 1.1 fusion.32
  10.3 4.1 %fusion.18 = (f32[64,4]{1,0:T(8,128)S(1)}, f32[64,2048]{1,0:T(8,128)S(1)}, f32[64,4]{1,0:T(8,128)S(1)}) fusion(bf16[64,4,2048]{2,1,0:T(4,128)(2,1)} %param.21, s32[64,4]{1,0:T(8,128)S(1)} %copy.25, pred[64,4]{1,0:T(8,128)(4,1)S(1)} %iota_compare_fusion.3, f32[64,4]{1,0:T(8,128)S(1)} %reduce_max.52), kind=kLoop, calls=%fused_computation.30 | loop fusion | flops 4062720 | bytes 1577216 | tf_op jit(solution)/shard_map/reduce_sum | solution.py:408
  14.5 43.2 %shard_map.131 = bf16[16,2,16,4608]{3,2,1,0:T(8,128)(2,1)S(1)} custom-call(bf16[16,4608]{1,0:T(8,128)(2,1)S(1)} %pad_maximum_fusion.9.x_ref), custom_call_target="tpu_custom_call" | custom-call | tf_op jit(solution)/shard_map/pallas_call | solution.py:118
  57.8 2.1 copy-done.2
  60.5 1.3 slice.182
  61.7 3.6 %slice_bitcast_fusion.4 = (bf16[256,3584]{1,0:T(8,128)(2,1)S(1)}, bf16[256,3584]{1,0:T(8,128)(2,1)}) fusion(bf16[32,16,4608]{2,1,0:T(8,128)(2,1)} %bitcast.48), kind=kLoop, calls=%fused_computation.36 | loop fusion | bytes 7340032 | tf_op jit(solution)/shard_map/reshape | solution.py:317
  65.3 1.3 reshape.199
  66.6 6.6 %fusion.4 = f32[320,512]{1,0:T(8,128)S(1)} fusion(bf16[1,7168,512]{2,1,0:T(8,128)(2,1)} %param.16, bf16[64,7168]{1,0:T(8,128)(2,1)} %reshape.199, bf16[256,3584]{1,0:T(8,128)(2,1)} %get-tuple-element.20, bf16[256,3584]{1,0:T(8,128)(2,1)S(1)} %get-tuple-element.19), kind=kOutput, calls=%fused_computation.5 | convolution fusion | flops 2362572800 | bytes 12582912 | tf_op jit(solution)/shard_map/dot_general | solution.py:375
  73.3 5.8 %fusion.23 = bf16[320,512]{1,0:T(8,128)(2,1)S(1)} fusion(bf16[1,7168,512]{2,1,0:T(8,128)(2,1)} %param.17, bf16[64,7168]{1,0:T(8,128)(2,1)S(1)} %copy-done.5, bf16[256,3584]{1,0:T(8,128)(2,1)S(1)} %copy-done.4, bf16[256,3584]{1,0:T(8,128)(2,1)S(1)} %get-tuple-element.19, f32[320,512]{1,0:T(8,128)S(1)} %fusion.4), kind=kOutput, calls=%fused_computation.38 | convolution fusion | flops 2363555840 | bytes 12910592 | tf_op jit(solution)/shard_map/dot_general | solution.py:376
  79.1 2.6 %fusion = bf16[320,7168]{1,0:T(8,128)(2,1)S(1)} fusion(bf16[320,512]{1,0:T(8,128)(2,1)S(1)} %fusion.23, bf16[1,512,7168]{2,1,0:T(8,128)(2,1)S(1)} %bitcast.63, f32[320]{0:T(512)S(1)} %pad_maximum_fusion.12), kind=kOutput, calls=%fused_computation.1 | convolution fusion | flops 2353397760 | bytes 12256512 | tf_op jit(solution)/shard_map/dot_general | solution.py:378
  81.8 2.0 slice_bitcast_fusion
  84.2 2.3 %fusion.55 = (bf16[32,8,3584]{2,1,0:T(8,128)(2,1)S(1)}, bf16[32,8,3584]{2,1,0:T(8,128)(2,1)S(1)}) fusion(bf16[32,8,7168]{2,1,0:T(8,128)(2,1)} %slice_bitcast_fusion), kind=kLoop, calls=%fused_computation.115 | loop fusion | bytes 7340032 | tf_op jit(solution)/shard_map/slice | solution.py:327
  87.4 36.9 %shard_map.132 = f32[16,4480]{1,0:T(8,128)S(1)} custom-call(bf16[16,2,16,4480]{3,2,1,0:T(8,128)(2,1)S(1)} %pad_maximum_fusion.1.p_ref), custom_call_target="tpu_custom_call" | custom-call | tf_op jit(solution)/shard_map/pallas_call | solution.py:230
  124.8 45.1 %shard_map.133 = bf16[16,2,16,4480]{3,2,1,0:T(8,128)(2,1)S(1)} custom-call(bf16[16,4480]{1,0:T(8,128)(2,1)S(1)} %pad_maximum_fusion.10.x_ref), custom_call_target="tpu_custom_call" | custom-call | tf_op jit(solution)/shard_map/pallas_call | solution.py:118
  170.0 2.1 slice_bitcast_fusion.2
  172.1 1.3 reshape.208
  173.4 18.7 %fusion.60 = (f32[320]{0:T(512)S(1)}, f32[320,2048]{1,0:T(8,128)S(1)}) fusion(bf16[2048,7168]{1,0:T(8,128)(2,1)} %param.20, bf16[64,7168]{1,0:T(8,128)(2,1)} %reshape.208, bf16[256,3584]{1,0:T(8,128)(2,1)} %get-tuple-element.22, bf16[256,3584]{1,0:T(8,128)(2,1)} %get-tuple-element.21), kind=kOutput, calls=%fused_computation.120 | convolution fusion | flops 9409658880 | bytes 36570368 | tf_op jit(solution)/shard_map/dot_general | solution.py:393
  193.8 11.8 %shard_map.134 = f32[32,16,128]{2,1,0:T(8,128)} custom-call(f32[16,128]{1,0:T(8,128)} %pad_bitcast_fusion.x_ref), custom_call_target="tpu_custom_call" | custom-call | tf_op jit(solution)/shard_map/pallas_call | solution.py:291
  208.7 2.9 %fusion.61 = (f32[64]{0:T(128)S(1)}, f32[64,2048]{1,0:T(8,128)}) fusion(f32[64]{0:T(128)S(1)} %broadcast_select_fusion, f32[64,2048]{1,0:T(8,128)S(1)} %get-tuple-element.9, f32[64]{0:T(128)S(1)} %get-tuple-element.17, pred[64]{0:T(512)(128)(4,1)} %broadcast_compare_fusion, f32[64]{0:T(128)} %get-tuple-element.16, f32[64]{0:T(128)} %get-tuple-element.15, ...), kind=kOutput, calls=%fused_computation.121 | convolution fusion | flops 504385472 | bytes 3672896 | tf_op jit(solution)/shard_map/dot_general | solution.py:435
  212.9 10.6 %shard_map.135 = f32[32,8,128]{2,1,0:T(8,128)} custom-call(f32[8,128]{1,0:T(8,128)} %pad_bitcast_fusion.1.x_ref), custom_call_target="tpu_custom_call" | custom-call | tf_op jit(solution)/shard_map/pallas_call | solution.py:291
  224.4 2.1 divide_sqrt_fusion
  (96 shorter events, 13.9 us)
Async XLA Ops:
  0.6 9.0 %copy-start = (bf16[7168,16]{0,1:T(8,128)(2,1)S(1)}, bf16[7168,16]{0,1:T(8,128)(2,1)}, u32[]{:S(2)}) copy-start(bf16[7168,16]{0,1:T(8,128)(2,1)} %param.14) | copy-start | bytes 688132
  57.8 2.1 copy-start.2
  66.6 6.6 %copy-start.4 = (bf16[256,3584]{1,0:T(8,128)(2,1)S(1)}, bf16[256,3584]{1,0:T(8,128)(2,1)}, u32[]{:S(2)}) copy-start(bf16[256,3584]{1,0:T(8,128)(2,1)} %get-tuple-element.20) | copy-start | bytes 5505028
  66.6 6.6 %copy-start.5 = (bf16[64,7168]{1,0:T(8,128)(2,1)S(1)}, bf16[64,7168]{1,0:T(8,128)(2,1)}, u32[]{:S(2)}) copy-start(bf16[64,7168]{1,0:T(8,128)(2,1)} %reshape.199) | copy-start | bytes 2752516
  66.6 12.5 %slice-start = ((s8[7340032]{0:T(1024)(128)(4,1)}), s8[4194304]{0:T(1024)(128)(4,1)S(1)}, s32[]{:S(2)}) async-start(s8[7340032]{0:T(1024)(128)(4,1)} %bitcast.62), calls=%async_computation | async-start | bytes 8388608
  73.2 5.9 %slice-start.1 = ((s8[7340032]{0:T(1024)(128)(4,1)}), s8[3145728]{0:T(1024)(128)(4,1)S(1)}, s32[]{:S(2)}) async-start(s8[7340032]{0:T(1024)(128)(4,1)} %bitcast.62), calls=%async_computation.1 | async-start | bytes 6291456
  87.4 37.0 %copy-start.3 = (bf16[10,7168]{1,0:T(8,128)(2,1)S(1)}, bf16[10,7168]{1,0:T(8,128)(2,1)}, u32[]{:S(2)}) copy-start(bf16[10,7168]{1,0:T(8,128)(2,1)} %param.12) | copy-start | bytes 430084
  87.4 37.2 %copy-start.6 = (f32[7168]{0:T(1024)S(1)}, f32[7168]{0:T(1024)}, u32[]{:S(2)}) copy-start(f32[7168]{0:T(1024)} %param.19) | copy-start | bytes 86020
  173.4 35.0 %copy-start.7 = (s32[64]{0:T(128)S(1)}, s32[64]{0:T(128)}, u32[]{:S(2)}) copy-start(s32[64]{0:T(128)} %param.23) | copy-start | bytes 772
  192.1 34.3 %copy-start.1 = (bf16[7168,16]{0,1:T(8,128)(2,1)S(1)}, bf16[7168,16]{0,1:T(8,128)(2,1)}, u32[]{:S(2)}) copy-start(bf16[7168,16]{0,1:T(8,128)(2,1)} %param.14) | copy-start | bytes 688132

commit v2 on v1

--- a/solution.py
+++ b/solution.py
@@ -13,6 +13,7 @@
 VMEM = pltpu.VMEM
 Z = 4
 CHIPS = 16
+LEVELS = (((0, 0),), ((0, 1), (1, 0)), ((1, 1),))
 CUT = 2304
 
 
@@ -49,9 +50,12 @@
     pl.semaphore_wait(barrier, 3 + (z + Z - 1) // Z + (2 * Z - 2 - z) // Z)
 
 
-def gather_kernel(width, x_ref, o_ref, send_sem, recv_sem):
+def gather_kernel(width, x_ref, rows_ref, *refs):
+    o_ref, pile, send_sem, recv_sem = refs[-4:]
     y, z, x, c = place()
     halves = (pl.ds(0, CUT), pl.ds(CUT, width - CUT))
+    half = rows_ref.shape[1] // 2
+    step = half // 4
     o_ref[y * 8 + z * 2 + x, c] = x_ref[...]
     greet()
 
@@ -68,7 +72,14 @@
 
     other = device(y, z, x, 1 - c)
 
-    def visit(k, drain):
+    def unpack(q):
+        one = o_ref[q, 0, :, :half].astype(jnp.float32)
+        two = o_ref[q, 1, :, :half].astype(jnp.float32)
+        to = pl.ds(pl.multiple_of(q * 16, 16), 16)
+        rows_ref[to, :half] = jnp.concatenate([one[:8], two[:8]], axis=0).astype(jnp.bfloat16)
+        rows_ref[to, half:] = jnp.concatenate([one[8:], two[8:]], axis=0).astype(jnp.bfloat16)
+
+    def visit(flips, drain, k):
         dz = offset_of(k)
         zs = z + dz
 
@@ -81,7 +92,7 @@
 
         @pl.when((zs >= 0) & (zs < Z))
         def _():
-            for fx, fy in ((0, 0), (0, 1), (1, 0), (1, 1)):
+            for fx, fy in flips:
                 q = (1 - y if fy else y) * 8 + zs * 2 + (1 - x if fx else x)
                 for h in (0, 1):
                     if not drain:
@@ -100,27 +111,46 @@
                     run(q, h, 0, other)
                     if drain:
                         copy(q, 1 - c, h, 0, other, 1).wait_recv()
-
-    @pl.loop(0, 2 * Z - 1)
-    def _(k):
-        visit(k, False)
-
-    @pl.loop(0, 2 * Z - 1)
-    def _(k):
-        visit(k, True)
-
-
-def gather(block, cid):
+                if drain:
+                    unpack(q)
+
+    for drain in (False, True):
+        for flips in LEVELS:
+            pl.loop(0, 2 * Z - 1)(functools.partial(visit, flips, drain))
+
+    @pl.loop(0, CHIPS // 4)
+    def _(g):
+        some = o_ref[pl.ds(g * 4, 4), :, :, half : half + step].astype(jnp.float32)
+        some = some.reshape(128, step)
+        to = pl.ds(pl.multiple_of(CHIPS * 16 + g * 16, 16), 16)
+        for i in range(step // 128):
+            pile[i] = some[:, i * 128 : (i + 1) * 128]
+            for j in range(8):
+                part = pile[i, pl.ds(j, 16, stride=8), :].astype(jnp.bfloat16)
+                rows_ref[to, j * step + i * 128 : j * step + (i + 1) * 128] = part
+
+    if len(refs) == 5:
+        refs[0][...] = o_ref[:, :, :, half + step :]
+
+
+def gather(block, width, cid):
     count = lax.axis_size("row") * lax.axis_size("vocab")
+    packed = width * 5 // 8
     if (lax.axis_size("row"), lax.axis_size("vocab")) != (2, 16):
-        return lax.all_gather(block, ("row", "vocab"), axis=0, tiled=False)
-    width = block.shape[1]
+        every = lax.all_gather(block, ("row", "vocab"), axis=0, tiled=False)
+        return spread(every, width), every[:, :, packed:]
+    extra = block.shape[1] - packed
+    shapes = [jax.ShapeDtypeStruct((count * 10, width), block.dtype)]
+    if extra:
+        shapes.append(jax.ShapeDtypeStruct((CHIPS, 2, 16, extra), block.dtype))
     out = pl.pallas_call(
-        functools.partial(gather_kernel, width),
-        out_shape=jax.ShapeDtypeStruct((CHIPS, 2, 16, width), block.dtype),
+        functools.partial(gather_kernel, block.shape[1]),
+        out_shape=shapes,
         in_specs=[pl.BlockSpec(memory_space=VMEM)],
-        out_specs=pl.BlockSpec(memory_space=VMEM),
+        out_specs=[pl.BlockSpec(memory_space=VMEM) for _ in shapes],
         scratch_shapes=[
+            VMEM((CHIPS, 2, 16, block.shape[1]), block.dtype),
+            VMEM((width // 1024, 128, 128), jnp.float32),
             pltpu.SemaphoreType.DMA((CHIPS, 2, 5)),
             pltpu.SemaphoreType.DMA((CHIPS, 2, 2)),
         ],
@@ -128,15 +158,37 @@
             collective_id=cid, has_side_effects=True, vmem_limit_bytes=40 * 2**20
         ),
     )(block)
-    return out.reshape(count, 16, width)
-
-
-def scatter_kernel(width, p_ref, o_ref, buf, stage, acc, send_sem, recv_sem):
+    return out[0], out[1].reshape(count, 16, extra) if extra else None
+
+
+def scatter_kernel(width, rows_ref, o_ref, p_ref, pile, buf, stage, acc, send_sem, recv_sem):
     y, z, x, c = place()
     halves = (pl.ds(0, CUT), pl.ds(CUT, width - CUT))
     sizes = (CUT, width - CUT)
     other = device(y, z, x, 1 - c)
+    half = rows_ref.shape[1] // 2
+    step = half // 4
+
+    @pl.loop(0, CHIPS // 4)
+    def _(g):
+        of = pl.ds(pl.multiple_of(CHIPS * 16 + g * 16, 16), 16)
+        for i in range(step // 128):
+            for j in range(8):
+                part = rows_ref[of, j * step + i * 128 : j * step + (i + 1) * 128]
+                pile[i, pl.ds(j, 16, stride=8), :] = part.astype(jnp.float32)
+            some = pile[i].reshape(4, 2, 16, 128).astype(jnp.bfloat16)
+            p_ref[pl.ds(g * 4, 4), :, :, half + i * 128 : half + (i + 1) * 128] = some
+
     greet()
+
+    def pack_chip(q):
+        of = pl.ds(pl.multiple_of(q * 16, 16), 16)
+        left = rows_ref[of, :half].astype(jnp.float32)
+        right = rows_ref[of, half:].astype(jnp.float32)
+        for core in (0, 1):
+            those = slice(core * 8, core * 8 + 8)
+            both = jnp.concatenate([left[those], right[those]], axis=0)
+            p_ref[q, core, :, :half] = both.astype(jnp.bfloat16)
 
     def chip(zs, fx, fy):
         return (1 - y if fy else y) * 8 + zs * 2 + (1 - x if fx else x)
@@ -161,9 +213,7 @@
             device_id_type=MESH,
         )
 
-    flips = ((1, 1), (1, 0), (0, 1), (0, 0))
-
-    def visit(i, phase):
+    def visit(flips, phase, i):
         dz = offset_of(2 * Z - 2 - i)
         zs = z + dz
 
@@ -171,6 +221,8 @@
         def _():
             for fx, fy in flips:
                 q = chip(zs, fx, fy)
+                if phase == 0:
+                    pack_chip(q)
                 for h in (0, 1):
                     if phase == 0:
                         to_core(q, h).start()
@@ -218,23 +270,26 @@
                         pl.when(dz < 0)(lambda: run(3, device(y, z - 1, x, c)))
 
     for phase in (0, 1, 2):
-        pl.loop(0, 2 * Z - 1)(functools.partial(lambda p, i: visit(i, p), phase))
-
-
-def scatter(parts, cid):
+        for flips in LEVELS[::-1]:
+            pl.loop(0, 2 * Z - 1)(functools.partial(visit, flips, phase))
+
+
+def scatter(rows, cid):
+    count = lax.axis_size("row") * lax.axis_size("vocab")
     if (lax.axis_size("row"), lax.axis_size("vocab")) != (2, 16):
-        return lax.psum_scatter(
-            parts.astype(jnp.float32), ("row", "vocab"), scatter_dimension=0, tiled=False
-        )
-    width = parts.shape[2]
+        parts = unspread(rows, count).astype(jnp.float32)
+        return lax.psum_scatter(parts, ("row", "vocab"), scatter_dimension=0, tiled=False)
+    packed = rows.shape[1] * 5 // 8
     return pl.pallas_call(
-        functools.partial(scatter_kernel, width),
-        out_shape=jax.ShapeDtypeStruct((16, width), jnp.float32),
+        functools.partial(scatter_kernel, packed),
+        out_shape=jax.ShapeDtypeStruct((16, packed), jnp.float32),
         in_specs=[pl.BlockSpec(memory_space=VMEM)],
         out_specs=pl.BlockSpec(memory_space=VMEM),
         scratch_shapes=[
-            VMEM((5, CHIPS, 16, width), jnp.bfloat16),
-            VMEM((CHIPS, 16, width), jnp.bfloat16),
+            VMEM((CHIPS, 2, 16, packed), jnp.bfloat16),
+            VMEM((rows.shape[1] // 1024, 128, 128), jnp.float32),
+            VMEM((5, CHIPS, 16, packed), jnp.bfloat16),
+            VMEM((CHIPS, 16, packed), jnp.bfloat16),
             VMEM((16, CUT), jnp.float32),
             pltpu.SemaphoreType.DMA((CHIPS, 2, 2)),
             pltpu.SemaphoreType.DMA((CHIPS, 2, 5)),
@@ -242,7 +297,7 @@
         compiler_params=pltpu.CompilerParams(
             collective_id=cid, has_side_effects=True, vmem_limit_bytes=40 * 2**20
         ),
-    )(parts.reshape(CHIPS, 2, 16, width))
+    )(rows)
 
 
 def exchange_kernel(n_vocab, count, x_ref, o_ref, send_sem, recv_sem):
@@ -351,7 +406,6 @@
     n_vocab = lax.axis_size("vocab")
     count = lax.axis_size("row") * n_vocab
     width = tokens.shape[1]
-    packed = width * 5 // 8
     experts = n_vocab
     resid_in = tokens.astype(jnp.float32)
     normed = rms_norm(resid_in, norm_gain).astype(jnp.bfloat16)
@@ -363,10 +417,9 @@
     low = weights - high
     both = jnp.concatenate([high, low], axis=1).astype(jnp.bfloat16)
     both = jnp.pad(both, ((0, 6), (0, 128 - 2 * experts)))
-    gathered = gather(jnp.concatenate([pack(normed), both], axis=1), 0)
-
-    x = spread(gathered, width)
-    table = gathered[:, :10, packed : packed + 2 * experts].astype(jnp.float32)
+    x, table = gather(jnp.concatenate([pack(normed), both], axis=1), width, 0)
+
+    table = table[:, :10, : 2 * experts].astype(jnp.float32)
     table = table[:, :, :experts] + table[:, :, experts:]
     mine = jnp.arange(experts, dtype=jnp.int32) == lax.axis_index("vocab")
     row_weight = jnp.sum(jnp.where(mine[None, None, :], table, 0.0), axis=-1)
@@ -377,7 +430,7 @@
     hidden = (jax.nn.silu(gate_out) * up_out).astype(jnp.bfloat16)
     down_out = jnp.dot(hidden, w_down[0], preferred_element_type=jnp.float32)
     parts = (down_out * row_weight[:, None]).astype(jnp.bfloat16)
-    summed = scatter(unspread(parts, count), 1)
+    summed = scatter(parts, 1)
 
     half = width // 2
     moe_sum = jnp.concatenate(
@@ -389,7 +442,7 @@
     )
     mixed_rows = resid_in + moe_sum
     final_normed = rms_norm(mixed_rows, head_gain).astype(jnp.bfloat16)
-    hn = spread(gather(pack(final_normed), 2), width)
+    hn, _ = gather(pack(final_normed), width, 2)
     logits = lax.dot_general(
         hn, head, (((1,), (1,)), ((), ())), preferred_element_type=jnp.float32
     )

time: 227 us -> 172 us (0.76)
  Pallas kernels: 148 us -> 108 us
  local copies, waits for them, and re-layouts: 23.3 us -> 11.1 us
  other arithmetic: 17.4 us -> 11.3 us
  matrix products: 36.9 us -> 40.7 us
    pallas_call x3, Pallas kernels: 125 us -> 85.5 us  [the longest x2 56 us: gather(): pl.pallas_call(functools.partial(gather_kernel, block.shape[1]), out_shap...]
    dot_general x1, matrix products: 2.56 us -> 13.6 us  [body(): down_out = jnp.dot(hidden, w_down[0], preferred_element_type=jnp.float32)]
    reshape x5 -> x0, local copies, waits for them, and re-layouts: 10.3 us -> none  [the longest x2 5.62 us: spread(): blocks[:, :8, :half].reshape(-1, half)]
    dot_general x1 -> x0, matrix products: 5.83 us -> none  [body(): up_out = jnp.dot(x, w_up[0], preferred_element_type=jnp.float32)]
    slice x4 -> x0, local copies, waits for them, and re-layouts: 3.68 us -> none  [the longest x1 2.29 us: unspread(): main = jnp.concatenate([first[:, :, :half], first[:, :, half:]], axis=1)]
    unnamed x25 -> x23, local copies, waits for them, and re-layouts: 5.66 us -> 7.87 us
where the time goes in v2:
time: 172 us
  Pallas kernels  108 us (63%)
  matrix products  40.7 us (24%)
  other arithmetic  11.3 us (7%)
  local copies, waits for them, and re-layouts  11.1 us (6%)
    pallas_call x2, Pallas kernels, gather(): pl.pallas_call(functools.partial(gather_kernel, block.shape[1]), out_shap...  56 us
    pallas_call x1, Pallas kernels, scatter(): pl.pallas_call(functools.partial(scatter_kernel, packed), out_shape=jax.S...  29.5 us
    pallas_call x2, Pallas kernels, exchange(): pl.pallas_call(functools.partial(exchange_kernel, n_vocab, count), out_sh...  22.4 us
    dot_general x1, matrix products, body(): lax.dot_general(hn, head, (((1,), (1,)), ((), ())), preferred_element_typ...  16.5 us
    dot_general x1, matrix products, body(): down_out = jnp.dot(hidden, w_down[0], preferred_element_type=jnp.float32)  13.6 us
    unnamed x23, local copies, waits for them, and re-layouts  7.87 us
    dot_general x1, matrix products, body(): gate_out = jnp.dot(x, w_gate[0], preferred_element_type=jnp.float32)  7 us

profile of v2, /device:TPU:0, one launch (start us, length us, event | category | flops | bytes accessed | tf_op | source)
XLA Modules:
  0.0 172.0 jit_solution(6243647397209499048)
XLA Ops:
  0.6 1.2 fusion.31
  1.8 1.1 fusion.33
  2.9 0.8 copy.21
  3.8 0.3 fusion.58
  4.4 29.2 %shard_map.131 = (bf16[320,7168]{1,0:T(8,128)(2,1)S(1)}, bf16[16,2,16,128]{3,2,1,0:T(8,128)(2,1)S(1)}) custom-call(bf16[16,4608]{1,0:T(8,128)(2,1)S(1)} %pad_maximum_fusion.x_ref), custom_call_target="tpu_custom_call" | custom-call | tf_op jit(solution)/shard_map/pallas_call | solution.py:146
  33.6 2.0 %copy-done.3 = bf16[320,7168]{1,0:T(8,128)(2,1)} copy-done((bf16[320,7168]{1,0:T(8,128)(2,1)}, bf16[320,7168]{1,0:T(8,128)(2,1)S(1)}, u32[]{:S(2)}) %copy-start.3) | copy-done | bytes 4587544
  36.2 7.0 %fusion.4 = f32[320,512]{1,0:T(8,128)S(1)} fusion(bf16[320,7168]{1,0:T(8,128)(2,1)} %copy-done.3, bf16[1,7168,512]{2,1,0:T(8,128)(2,1)} %param.16), kind=kOutput, calls=%fused_computation.5 | convolution fusion | flops 2348810240 | bytes 12582912 | tf_op jit(solution)/shard_map/dot_general | solution.py:428
  43.2 13.6 %fusion.rows_ref = bf16[320,7168]{1,0:T(8,128)(2,1)} fusion(bf16[1,512,7168]{2,1,0:T(8,128)(2,1)} %param.18, f32[320]{0:T(512)S(1)} %pad_maximum_fusion.3, bf16[320,7168]{1,0:T(8,128)(2,1)} %copy-done.3, bf16[1,7168,512]{2,1,0:T(8,128)(2,1)} %param.17, f32[320,512]{1,0:T(8,128)S(1)} %fusion.4), kind=kOutput, calls=%fused_computation.1 | convolution fusion | flops 4703191040 | bytes 24511744 | tf_op jit(solution)/shard_map/dot_general | solution.py:431
  56.8 2.3 %copy-done.2 = bf16[320,7168]{1,0:T(8,128)(2,1)S(1)} copy-done((bf16[320,7168]{1,0:T(8,128)(2,1)S(1)}, bf16[320,7168]{1,0:T(8,128)(2,1)}, u32[]{:S(2)}) %copy-start.2) | copy-done | bytes 4587544
  59.1 29.5 %shard_map.132 = f32[16,4480]{1,0:T(8,128)S(1)} custom-call(bf16[320,7168]{1,0:T(8,128)(2,1)S(1)} %copy-done.2), custom_call_target="tpu_custom_call" | custom-call | tf_op jit(solution)/shard_map/pallas_call | solution.py:283
  89.2 26.8 %shard_map.133 = bf16[320,7168]{1,0:T(8,128)(2,1)S(1)} custom-call(bf16[16,4480]{1,0:T(8,128)(2,1)S(1)} %pad_maximum_fusion.1.x_ref), custom_call_target="tpu_custom_call" | custom-call | tf_op jit(solution)/shard_map/pallas_call | solution.py:146
  116.0 16.5 %fusion.59 = (f32[320]{0:T(512)S(1)}, f32[320,2048]{1,0:T(8,128)}) fusion(bf16[320,7168]{1,0:T(8,128)(2,1)S(1)} %shard_map.133, bf16[2048,7168]{1,0:T(8,128)(2,1)} %param.20), kind=kOutput, calls=%fused_computation.109 | convolution fusion | flops 9395896320 | bytes 36570368 | tf_op jit(solution)/shard_map/dot_general | solution.py:446
  133.0 2.7 %select_reduce_fusion = (f32[320]{0:T(512)S(1)}, f32[320]{0:T(512)S(1)}) fusion(f32[320,2048]{1,0:T(8,128)} %get-tuple-element.35, s32[320]{0:T(512)S(1)} %pad_add_fusion.1, f32[320]{0:T(512)S(1)} %get-tuple-element.34), kind=kLoop, calls=%fused_computation.10 | loop fusion | flops 3276160 | bytes 2626560 | tf_op jit(solution)/shard_map/reduce_sum | solution.py:460
  135.7 0.5 reduce_max.46
  136.3 3.1 %fusion.12 = (f32[64,4]{1,0:T(8,128)S(1)}, f32[64,2048]{1,0:T(8,128)S(1)}, f32[64,4]{1,0:T(8,128)S(1)}) fusion(bf16[64,4,2048]{2,1,0:T(4,128)(2,1)S(1)} %copy-done.4, s32[64,4]{1,0:T(8,128)S(1)} %copy.25, pred[64,4]{1,0:T(8,128)(4,1)S(1)} %iota_compare_fusion.3, f32[64,4]{1,0:T(8,128)S(1)} %reduce_max.52), kind=kLoop, calls=%fused_computation.20 | loop fusion | flops 4062720 | bytes 1577216 | tf_op jit(solution)/shard_map/reduce_sum | solution.py:461
  139.8 0.6 pad_bitcast_fusion.x_ref
  140.4 12.1 %shard_map.134 = f32[32,16,128]{2,1,0:T(8,128)} custom-call(f32[16,128]{1,0:T(8,128)} %pad_bitcast_fusion.x_ref), custom_call_target="tpu_custom_call" | custom-call | tf_op jit(solution)/shard_map/pallas_call | solution.py:346
  152.5 1.0 copy.30
  155.3 3.2 %fusion.60 = (f32[64]{0:T(128)S(1)}, f32[64,2048]{1,0:T(8,128)S(1)}) fusion(f32[64]{0:T(128)S(1)} %broadcast_select_fusion, f32[64,2048]{1,0:T(8,128)S(1)} %get-tuple-element.13, f32[64]{0:T(128)S(1)} %get-tuple-element.21, pred[64]{0:T(512)(128)(4,1)S(1)} %broadcast_compare_fusion, f32[64]{0:T(128)S(1)} %get-tuple-element.20, ...), kind=kOutput, calls=%fused_computation.110 | convolution fusion | flops 504385472 | bytes 3672896 | tf_op jit(solution)/shard_map/dot_general | solution.py:488
  158.5 0.6 pad_bitcast_fusion.1.x_ref
  159.1 10.3 %shard_map.135 = f32[32,8,128]{2,1,0:T(8,128)} custom-call(f32[8,128]{1,0:T(8,128)} %pad_bitcast_fusion.1.x_ref), custom_call_target="tpu_custom_call" | custom-call | tf_op jit(solution)/shard_map/pallas_call | solution.py:346
  169.4 0.9 copy.31
  170.4 1.0 divide_sqrt_fusion
  171.4 0.7 copy.24
  (80 shorter events, 4.0 us)
Async XLA Ops:
  0.6 3.1 %copy-start = (bf16[7168,16]{0,1:T(8,128)(2,1)S(1)}, bf16[7168,16]{0,1:T(8,128)(2,1)}, u32[]{:S(2)}) copy-start(bf16[7168,16]{0,1:T(8,128)(2,1)} %param.14) | copy-start | bytes 688132
  33.6 2.1 %copy-start.3 = (bf16[320,7168]{1,0:T(8,128)(2,1)}, bf16[320,7168]{1,0:T(8,128)(2,1)S(1)}, u32[]{:S(2)}) copy-start(bf16[320,7168]{1,0:T(8,128)(2,1)S(1)} %get-tuple-element.4) | copy-start | bytes 13762564
  56.8 2.3 %copy-start.2 = (bf16[320,7168]{1,0:T(8,128)(2,1)S(1)}, bf16[320,7168]{1,0:T(8,128)(2,1)}, u32[]{:S(2)}) copy-start(bf16[320,7168]{1,0:T(8,128)(2,1)} %fusion.rows_ref) | copy-start | bytes 13762564
  59.1 29.6 %copy-start.5 = (bf16[10,7168]{1,0:T(8,128)(2,1)S(1)}, bf16[10,7168]{1,0:T(8,128)(2,1)}, u32[]{:S(2)}) copy-start(bf16[10,7168]{1,0:T(8,128)(2,1)} %param.12) | copy-start | bytes 430084
  59.1 29.8 %copy-start.6 = (f32[7168]{0:T(1024)S(1)}, f32[7168]{0:T(1024)}, u32[]{:S(2)}) copy-start(f32[7168]{0:T(1024)} %param.19) | copy-start | bytes 86020
  116.0 16.6 %copy-start.8 = (s32[64,4]{0,1:T(4,128)S(1)}, s32[64,4]{0,1:T(4,128)}, u32[]{:S(2)}) copy-start(s32[64,4]{0,1:T(4,128)} %param.22) | copy-start | bytes 3076
  116.0 19.7 %copy-start.4 = (bf16[64,4,2048]{2,1,0:T(4,128)(2,1)S(1)}, bf16[64,4,2048]{2,1,0:T(4,128)(2,1)}, u32[]{:S(2)}) copy-start(bf16[64,4,2048]{2,1,0:T(4,128)(2,1)} %param.21) | copy-start | bytes 3145732
  116.0 20.2 %copy-start.7 = (s32[64]{0:T(128)S(1)}, s32[64]{0:T(128)}, u32[]{:S(2)}) copy-start(s32[64]{0:T(128)} %param.23) | copy-start | bytes 772
  136.2 35.8 %copy-start.1 = (bf16[7168,16]{0,1:T(8,128)(2,1)S(1)}, bf16[7168,16]{0,1:T(8,128)(2,1)}, u32[]{:S(2)}) copy-start(bf16[7168,16]{0,1:T(8,128)(2,1)} %param.14) | copy-start | bytes 688132

commit v3 on v2

--- a/solution.py
+++ b/solution.py
@@ -355,6 +355,83 @@
         compiler_params=pltpu.CompilerParams(collective_id=cid, has_side_effects=True),
     )(block)
     return out.reshape(count, rows * 128)[:, :size]
+
+
+def hidden_kernel(x_ref, gate_ref, up_ref, o_ref, gate_sum, up_sum):
+    step = pl.program_id(0)
+
+    @pl.when(step == 0)
+    def _():
+        gate_sum[...] = jnp.zeros_like(gate_sum)
+        up_sum[...] = jnp.zeros_like(up_sum)
+
+    x = x_ref[...]
+    gate_sum[...] += jnp.dot(x, gate_ref[...], preferred_element_type=jnp.float32)
+    up_sum[...] += jnp.dot(x, up_ref[...], preferred_element_type=jnp.float32)
+
+    @pl.when(step == pl.num_programs(0) - 1)
+    def _():
+        gate = gate_sum[...]
+        o_ref[...] = (gate / (1.0 + jnp.exp(-gate)) * up_sum[...]).astype(jnp.bfloat16)
+
+
+def hidden_units(x, gate_w, up_w):
+    rows, width = x.shape
+    units = gate_w.shape[1]
+    if (lax.axis_size("row"), lax.axis_size("vocab")) != (2, 16):
+        gate_out = jnp.dot(x, gate_w, preferred_element_type=jnp.float32)
+        up_out = jnp.dot(x, up_w, preferred_element_type=jnp.float32)
+        return (jax.nn.silu(gate_out) * up_out).astype(jnp.bfloat16)
+    depth = width // 7
+    return pl.pallas_call(
+        hidden_kernel,
+        out_shape=jax.ShapeDtypeStruct((rows, units), jnp.bfloat16),
+        grid=(7,),
+        in_specs=[
+            pl.BlockSpec((rows, depth), lambda i: (0, i)),
+            pl.BlockSpec((depth, units), lambda i: (i, 0)),
+            pl.BlockSpec((depth, units), lambda i: (i, 0)),
+        ],
+        out_specs=pl.BlockSpec((rows, units), lambda i: (0, 0)),
+        scratch_shapes=[VMEM((rows, units), jnp.float32), VMEM((rows, units), jnp.float32)],
+        compiler_params=pltpu.CompilerParams(vmem_limit_bytes=40 * 2**20),
+        cost_estimate=pl.CostEstimate(
+            flops=4 * rows * width * units,
+            bytes_accessed=2 * width * (2 * units + rows),
+            transcendentals=rows * units,
+        ),
+    )(x, gate_w, up_w)
+
+
+def head_kernel(x_ref, head_ref, o_ref):
+    o_ref[...] = lax.dot_general(
+        x_ref[...], head_ref[...], (((1,), (1,)), ((), ())), preferred_element_type=jnp.float32
+    )
+
+
+def head_logits(x, head):
+    rows, width = x.shape
+    entries = head.shape[0]
+    if (lax.axis_size("row"), lax.axis_size("vocab")) != (2, 16):
+        return lax.dot_general(
+            x, head, (((1,), (1,)), ((), ())), preferred_element_type=jnp.float32
+        )
+    return pl.pallas_call(
+        head_kernel,
+        out_shape=jax.ShapeDtypeStruct((rows, entries), jnp.float32),
+        grid=(entries // 256,),
+        in_specs=[
+            pl.BlockSpec((rows, width), lambda i: (0, 0)),
+            pl.BlockSpec((256, width), lambda i: (i, 0)),
+        ],
+        out_specs=pl.BlockSpec((rows, 256), lambda i: (0, i)),
+        compiler_params=pltpu.CompilerParams(vmem_limit_bytes=40 * 2**20),
+        cost_estimate=pl.CostEstimate(
+            flops=2 * rows * width * entries,
+            bytes_accessed=2 * width * (entries + rows) + 4 * rows * entries,
+            transcendentals=0,
+        ),
+    )(x, head)
 
 
 def pack(rows):
@@ -425,9 +502,7 @@
     row_weight = jnp.sum(jnp.where(mine[None, None, :], table, 0.0), axis=-1)
     row_weight = in_order(row_weight.reshape(-1), count)
 
-    gate_out = jnp.dot(x, w_gate[0], preferred_element_type=jnp.float32)
-    up_out = jnp.dot(x, w_up[0], preferred_element_type=jnp.float32)
-    hidden = (jax.nn.silu(gate_out) * up_out).astype(jnp.bfloat16)
+    hidden = hidden_units(x, w_gate[0], w_up[0])
     down_out = jnp.dot(hidden, w_down[0], preferred_element_type=jnp.float32)
     parts = (down_out * row_weight[:, None]).astype(jnp.bfloat16)
     summed = scatter(parts, 1)
@@ -443,9 +518,7 @@
     mixed_rows = resid_in + moe_sum
     final_normed = rms_norm(mixed_rows, head_gain).astype(jnp.bfloat16)
     hn, _ = gather(pack(final_normed), width, 2)
-    logits = lax.dot_general(
-        hn, head, (((1,), (1,)), ((), ())), preferred_element_type=jnp.float32
-    )
+    logits = head_logits(hn, head)
 
     local_vocab = head.shape[0]
     requests = draft_tokens.shape[0]

time: 172 us -> 167 us (0.971)
  matrix products: 40.7 us -> 5.4 us
  Pallas kernels: 108 us -> 133 us
  local copies, waits for them, and re-layouts: 11.1 us -> 14.6 us
    pallas_call x0 -> x2, Pallas kernels: none -> 24.8 us  [the longest x1 15.5 us: head_logits(): pl.pallas_call(head_kernel, out_shape=jax.ShapeDtypeStruct((rows, entries...]
    dot_general x2 -> x0, matrix products: 23.5 us -> none  [the longest x1 16.5 us: body(): lax.dot_general(hn, head, (((1,), (1,)), ((), ())), preferred_element_typ...]
    dot_general x1, matrix products: 13.6 us -> 2.56 us  [body(): down_out = jnp.dot(hidden, w_down[0], preferred_element_type=jnp.float32)]
    unnamed x23 -> x25, local copies, waits for them, and re-layouts: 7.87 us -> 11.4 us
    reduce_sum x1, other arithmetic: 3.07 us -> 4.86 us  [body(): jnp.sum(jnp.where(lanes[None, None, :] == local_ids[:, :, None], draft_va...]
    reduce_sum x1, other arithmetic: 2.69 us -> 0.96 us  [body(): jnp.sum(jnp.where(lanes[None, :] == row_ids[:, None], logits, 0.0), axis=-1)]
where the time goes in v3:
time: 167 us
  Pallas kernels  133 us (80%)
  local copies, waits for them, and re-layouts  14.6 us (9%)
  other arithmetic  12.8 us (8%)
  matrix products  5.4 us (3%)
    pallas_call x2, Pallas kernels, gather(): pl.pallas_call(functools.partial(gather_kernel, block.shape[1]), out_shap...  56 us
    pallas_call x1, Pallas kernels, scatter(): pl.pallas_call(functools.partial(scatter_kernel, packed), out_shape=jax.S...  29.6 us
    pallas_call x2, Pallas kernels, exchange(): pl.pallas_call(functools.partial(exchange_kernel, n_vocab, count), out_sh...  22.4 us
    pallas_call x1, Pallas kernels, head_logits(): pl.pallas_call(head_kernel, out_shape=jax.ShapeDtypeStruct((rows, entries...  15.5 us
    unnamed x25, local copies, waits for them, and re-layouts  11.4 us
    pallas_call x1, Pallas kernels, hidden_units(): pl.pallas_call(hidden_kernel, out_shape=jax.ShapeDtypeStruct((rows, units...  9.23 us
    reduce_sum x1, other arithmetic, body(): jnp.sum(jnp.where(lanes[None, None, :] == local_ids[:, :, None], draft_va...  4.86 us

profile of v3, /device:TPU:0, one launch (start us, length us, event | category | flops | bytes accessed | tf_op | source)
XLA Modules:
  0.0 166.6 jit_solution(1321941967962940085)
XLA Ops:
  0.6 1.2 fusion.14
  1.8 1.1 fusion.16
  2.9 0.8 copy.21
  4.4 29.2 %shard_map.131 = (bf16[320,7168]{1,0:T(8,128)(2,1)S(1)}, bf16[16,2,16,128]{3,2,1,0:T(8,128)(2,1)S(1)}) custom-call(bf16[16,4608]{1,0:T(8,128)(2,1)S(1)} %pad_maximum_fusion.x_ref), custom_call_target="tpu_custom_call" | custom-call | tf_op jit(solution)/shard_map/pallas_call | solution.py:146
  33.6 2.0 %copy-done.3 = bf16[320,7168]{1,0:T(8,128)(2,1)} copy-done((bf16[320,7168]{1,0:T(8,128)(2,1)}, bf16[320,7168]{1,0:T(8,128)(2,1)S(1)}, u32[]{:S(2)}) %copy-start.3) | copy-done | bytes 4587544
  36.2 3.1 %copy-done.2 = bf16[1,7168,512]{2,1,0:T(8,128)(2,1)S(1)} copy-done((bf16[1,7168,512]{2,1,0:T(8,128)(2,1)S(1)}, bf16[1,7168,512]{2,1,0:T(8,128)(2,1)}, u32[]{:S(2)}) %copy-start.2) | copy-done | bytes 7340056
  39.3 2.3 %copy-done.4 = bf16[320,7168]{1,0:T(8,128)(2,1)S(1)} copy-done((bf16[320,7168]{1,0:T(8,128)(2,1)S(1)}, bf16[320,7168]{1,0:T(8,128)(2,1)}, u32[]{:S(2)}) %copy-start.4) | copy-done | bytes 4587544
  41.6 9.2 %shard_map.132 = bf16[320,512]{1,0:T(8,128)(2,1)S(1)} custom-call(bf16[320,7168]{1,0:T(8,128)(2,1)S(1)} %copy-done.4, bf16[7168,512]{1,0:T(8,128)(2,1)S(1)} %bitcast.25, bf16[7168,512]{1,0:T(8,128)(2,1)} %bitcast.27), custom_call_target="tpu_custom_call" | custom-call | flops 4697620480 | bytes 19267584 | tf_op jit(solution)/shard_map/pallas_call | solution.py:386
  50.8 2.6 %fusion.rows_ref = bf16[320,7168]{1,0:T(8,128)(2,1)S(1)} fusion(bf16[320,512]{1,0:T(8,128)(2,1)S(1)} %shard_map.132, bf16[1,512,7168]{2,1,0:T(8,128)(2,1)S(1)} %copy-done.9, f32[320]{0:T(512)S(1)} %pad_maximum_fusion.3), kind=kOutput, calls=%fused_computation.1 | convolution fusion | flops 2353397760 | bytes 12256512 | tf_op jit(solution)/shard_map/dot_general | solution.py:506
  53.4 29.6 %shard_map.133 = f32[16,4480]{1,0:T(8,128)S(1)} custom-call(bf16[320,7168]{1,0:T(8,128)(2,1)S(1)} %fusion.rows_ref), custom_call_target="tpu_custom_call" | custom-call | tf_op jit(solution)/shard_map/pallas_call | solution.py:283
  83.5 26.8 %shard_map.134.x_ref = bf16[320,7168]{1,0:T(8,128)(2,1)S(1)} custom-call(bf16[16,4480]{1,0:T(8,128)(2,1)S(1)} %pad_maximum_fusion.1.x_ref), custom_call_target="tpu_custom_call" | custom-call | tf_op jit(solution)/shard_map/pallas_call | solution.py:146
  110.3 15.5 %shard_map.135 = f32[320,2048]{1,0:T(8,128)S(1)} custom-call(bf16[320,7168]{1,0:T(8,128)(2,1)S(1)} %shard_map.134.x_ref, bf16[2048,7168]{1,0:T(8,128)(2,1)} %head_ref.1), custom_call_target="tpu_custom_call" | custom-call | flops 9395240960 | bytes 36569088 | tf_op jit(solution)/shard_map/pallas_call | solution.py:419
  127.0 1.0 select_reduce_fusion
  128.0 1.7 %reduce_max.46 = bf16[64,4]{1,0:T(8,128)(2,1)S(1)} reduce(bf16[64,4,2048]{2,1,0:T(4,128)(2,1)} %param.21, bf16[]{:T(256)} %constant.48.clone.1), dimensions={2}, to_apply=%region_8.9 | reduce | flops 524032 | bytes 1049090 | tf_op jit(solution)/shard_map/reduce_max | solution.py:538
  129.8 4.9 %fusion.8 = (f32[64,4]{1,0:T(8,128)S(1)}, f32[64,2048]{1,0:T(8,128)}, f32[64,4]{1,0:T(8,128)S(1)}) fusion(bf16[64,4,2048]{2,1,0:T(4,128)(2,1)} %param.21, s32[64,4]{1,0:T(8,128)S(1)} %copy.25, pred[64,4]{1,0:T(8,128)(4,1)S(1)} %iota_compare_fusion.3, f32[64,4]{1,0:T(8,128)S(1)} %reduce_max.52), kind=kLoop, calls=%fused_computation.16 | loop fusion | flops 4062720 | bytes 1577216 | tf_op jit(solution)/shard_map/reduce_sum | solution.py:534
  135.1 0.6 pad_bitcast_fusion.x_ref
  135.7 12.1 %shard_map.136 = f32[32,16,128]{2,1,0:T(8,128)} custom-call(f32[16,128]{1,0:T(8,128)} %pad_bitcast_fusion.x_ref), custom_call_target="tpu_custom_call" | custom-call | tf_op jit(solution)/shard_map/pallas_call | solution.py:346
  147.8 1.0 copy.30
  150.6 2.5 %fusion.40 = (f32[64]{0:T(128)S(1)}, f32[64,2048]{1,0:T(8,128)S(1)}) fusion(f32[64]{0:T(128)S(1)} %broadcast_select_fusion, f32[64,2048]{1,0:T(8,128)} %get-tuple-element.13, f32[64]{0:T(128)S(1)} %get-tuple-element.21, pred[64]{0:T(512)(128)(4,1)S(1)} %broadcast_compare_fusion, f32[64]{0:T(128)S(1)} %get-tuple-element.20, f32[64]{0:T(128)S(1)} %get-tuple-element.19, ...), kind=kOutput, calls=%fused_computation.96 | convolution fusion | flops 504385472 | bytes 3672896 | tf_op jit(solution)/shard_map/dot_general | solution.py:561
  153.1 0.6 pad_bitcast_fusion.1.x_ref
  153.7 10.3 %shard_map.137 = f32[32,8,128]{2,1,0:T(8,128)} custom-call(f32[8,128]{1,0:T(8,128)} %pad_bitcast_fusion.1.x_ref), custom_call_target="tpu_custom_call" | custom-call | tf_op jit(solution)/shard_map/pallas_call | solution.py:346
  164.0 0.9 copy.31
  165.0 1.0 divide_sqrt_fusion
  166.0 0.7 copy.24
  (83 shorter events, 5.0 us)
Async XLA Ops:
  0.6 3.1 %copy-start = (bf16[7168,16]{0,1:T(8,128)(2,1)S(1)}, bf16[7168,16]{0,1:T(8,128)(2,1)}, u32[]{:S(2)}) copy-start(bf16[7168,16]{0,1:T(8,128)(2,1)} %param.14) | copy-start | bytes 688132
  33.6 2.1 %copy-start.3 = (bf16[320,7168]{1,0:T(8,128)(2,1)}, bf16[320,7168]{1,0:T(8,128)(2,1)S(1)}, u32[]{:S(2)}) copy-start(bf16[320,7168]{1,0:T(8,128)(2,1)S(1)} %get-tuple-element.4.x_ref) | copy-start | bytes 13762564
  36.2 3.1 %copy-start.2 = (bf16[1,7168,512]{2,1,0:T(8,128)(2,1)S(1)}, bf16[1,7168,512]{2,1,0:T(8,128)(2,1)}, u32[]{:S(2)}) copy-start(bf16[1,7168,512]{2,1,0:T(8,128)(2,1)} %param.16) | copy-start | bytes 22020100
  39.3 2.3 %copy-start.4 = (bf16[320,7168]{1,0:T(8,128)(2,1)S(1)}, bf16[320,7168]{1,0:T(8,128)(2,1)}, u32[]{:S(2)}) copy-start(bf16[320,7168]{1,0:T(8,128)(2,1)} %copy-done.3) | copy-start | bytes 13762564
  41.6 9.2 %copy-start.9 = (bf16[1,512,7168]{2,1,0:T(8,128)(2,1)S(1)}, bf16[1,512,7168]{2,1,0:T(8,128)(2,1)}, u32[]{:S(2)}) copy-start(bf16[1,512,7168]{2,1,0:T(8,128)(2,1)} %param.18) | copy-start | bytes 22020100
  53.4 29.7 %copy-start.5 = (bf16[10,7168]{1,0:T(8,128)(2,1)S(1)}, bf16[10,7168]{1,0:T(8,128)(2,1)}, u32[]{:S(2)}) copy-start(bf16[10,7168]{1,0:T(8,128)(2,1)} %param.12) | copy-start | bytes 430084
  53.4 29.9 %copy-start.6 = (f32[7168]{0:T(1024)S(1)}, f32[7168]{0:T(1024)}, u32[]{:S(2)}) copy-start(f32[7168]{0:T(1024)} %param.19) | copy-start | bytes 86020
  125.9 0.7 copy-start.8
  126.1 3.6 %copy-start.7 = (s32[64]{0:T(128)S(1)}, s32[64]{0:T(128)}, u32[]{:S(2)}) copy-start(s32[64]{0:T(128)} %param.23) | copy-start | bytes 772
  150.5 16.1 %copy-start.1 = (bf16[7168,16]{0,1:T(8,128)(2,1)S(1)}, bf16[7168,16]{0,1:T(8,128)(2,1)}, u32[]{:S(2)}) copy-start(bf16[7168,16]{0,1:T(8,128)(2,1)} %param.14) | copy-start | bytes 688132
